TPU v7x, 32 devices: a whole 2x2x4 slice. The times are simulated.
32 devices in a mesh: seq: 4 (over z), files: 8 (over y, x, core).
Axes of the slice: x: 2, y: 2, z: 4, core: 2. Of those that a mesh axis runs over, the one named last changes fastest.
Arguments:
- q_lin: bfloat16 [8, 1024, 320], P('files', 'seq'), may hold values from -6 to 6
- k_lin: bfloat16 [8, 1024, 320], P('files', 'seq'), may hold values from -6 to 6
- v_lin: bfloat16 [8, 1024, 2560], P('files', 'seq'), may hold values from -6 to 6
- q_soft: bfloat16 [8, 1024, 1280], P('files', 'seq'), may hold values from -48 to 48
- k_soft: bfloat16 [8, 1024, 1280], P('files', 'seq'), may hold values from -6 to 6
- v_soft: bfloat16 [8, 1024, 1280], P('files', 'seq'), may hold values from -6 to 6
- import_ids: int32 [8, 4, 2], P('files', 'seq'), may hold values from -1 to 15, as said below
- import_counts: int32 [8, 4], P('files', 'seq'), may hold values from 1 to 2, as said below
Outputs:
- lin_out: bfloat16 [8, 1024, 2560], P('files', 'seq')
- soft_out: bfloat16 [8, 1024, 1280], P('files', 'seq')
Inputs may be any that keep to these rules, and one draw needn't show every extreme that they name: `import_ids`: entries before the count name distinct file groups other than the reader's own, entry = group * 2 + block; entries from the count on are -1. For each sequence shard index, some file group is listed before the count by every other file group's list of that index. `import_counts`: some sequence shard lists 2 blocks.
All inputs are finite; a program needn't handle non-finite values.
Results may differ from a plain program's by a relative error of at most 0.005.
Values may be sent and summed in bfloat16 or wider, within the bound.
A program may use at most 192 MiB of HBM per device.

v0:
```python
import math

import jax
import jax.numpy as jnp
import numpy as np
from jax import lax
from jax.sharding import PartitionSpec as P

D = 2560
HEADS = 20
FEAT = 16
FEATS = 153
SM_HEADS = 10
SM_HD = 128
SM_W = 1280
BLK = 128


inv_root_two = 0.7071067811865476
highest_precision = lax.Precision.HIGHEST


def entering(part, axis, combine, identity):
    place = lax.axis_index(axis)
    gathered = jax.tree.map(lambda a: lax.all_gather(a, axis), part)
    state = jax.tree.map(lambda a, e: jnp.zeros_like(a) + jnp.asarray(e, a.dtype), part, identity)

    def one(lap, state):
        return combine(
            state, jax.tree.map(lambda a: lax.dynamic_index_in_dim(a, lap, 0, False), gathered)
        )

    return lax.fori_loop(0, place, one, state)


def feature_map(inputs):
    count_in = inputs.shape[-1]
    rows, cols = np.triu_indices(count_in)
    factor = np.where(rows == cols, inv_root_two, 1.0).astype(np.float32)
    quadratic = inputs[..., rows] * inputs[..., cols] * factor
    ones = jnp.ones(inputs.shape[:-1] + (1,), inputs.dtype)
    return jnp.concatenate([ones, inputs, quadratic], axis=-1)


def exclusive(values):
    shifted = jnp.concatenate([jnp.zeros_like(values[:1]), values[:-1]], axis=0)
    return jnp.cumsum(shifted, axis=0)


def add_pairs(earlier, later):
    return (earlier[0] + later[0], earlier[1] + later[1])


def carried_prefix(running_state, norm_sum):
    empty = (jnp.zeros_like(running_state), jnp.zeros_like(norm_sum))
    return entering((running_state, norm_sum), "seq", add_pairs, empty)


def linear_layer(query_rows, key_rows, value_rows, tokens, blocks):
    head_dim = D // HEADS
    causal_masking = jnp.tril(jnp.ones((BLK, BLK), jnp.float32))
    feat_q = feature_map(query_rows.astype(jnp.float32).reshape(tokens, HEADS, FEAT) * 0.5).astype(
        jnp.bfloat16
    )
    feat_k = feature_map(key_rows.astype(jnp.float32).reshape(tokens, HEADS, FEAT) * 0.5).astype(
        jnp.bfloat16
    )
    feat_q = feat_q.reshape(blocks, BLK, HEADS, FEATS)
    feat_k = feat_k.reshape(blocks, BLK, HEADS, FEATS)
    values = value_rows.reshape(blocks, BLK, HEADS, head_dim)
    weight_matrix = (
        jnp.einsum("bqhf,bkhf->bhqk", feat_q, feat_k, preferred_element_type=jnp.float32)
        * causal_masking
    )
    local_num = jnp.einsum(
        "bhqk,bkhd->bqhd",
        weight_matrix.astype(jnp.bfloat16),
        values,
        preferred_element_type=jnp.float32,
    )
    block_states = jnp.einsum("bkhf,bkhd->bhfd", feat_k, values, preferred_element_type=jnp.float32)
    block_norms = jnp.sum(feat_k.astype(jnp.float32), axis=1)
    carried_state, carried_norm = carried_prefix(
        jnp.sum(block_states, axis=0), jnp.sum(block_norms, axis=0)
    )
    state_in = carried_state[None] + exclusive(block_states)
    norm_in = carried_norm[None] + exclusive(block_norms)
    feat_q32 = feat_q.astype(jnp.float32)
    carried_term = jnp.einsum("bqhf,bhfd->bqhd", feat_q32, state_in, precision=highest_precision)
    denominator = jnp.transpose(jnp.sum(weight_matrix, axis=-1), (0, 2, 1))
    denominator = denominator + jnp.einsum(
        "bqhf,bhf->bqh", feat_q32, norm_in, precision=highest_precision
    )
    output = (local_num + carried_term) / denominator[..., None]
    return output.astype(jnp.bfloat16).reshape(1, tokens, D)


def owner_selection(import_ids, import_counts, blocks):
    groups = lax.axis_size("files")
    list_len = import_ids.shape[2]
    id_row = import_ids[0, 0]
    listed = jnp.arange(list_len) < import_counts[0, 0]
    table = (jnp.arange(groups)[:, None] == id_row[None, :] // blocks) & listed[None, :]
    codes = jnp.sum(jnp.where(table, id_row[None, :] % blocks + 1, 0), axis=1)
    local_code = lax.all_to_all(
        codes.reshape(groups, 1), "files", split_axis=0, concat_axis=0, tiled=True
    )[:, 0]
    return (jnp.arange(blocks)[None, :] + 1 == local_code[:, None]).astype(jnp.bfloat16)


def softmax_layer(q_soft, k_soft, v_soft, import_ids, import_counts, tokens, blocks):
    groups = lax.axis_size("files")
    list_len = import_ids.shape[2]
    scale = 1.0 / math.sqrt(SM_HD)
    selection = owner_selection(import_ids, import_counts, blocks)
    key_blocks = k_soft[0].reshape(blocks, BLK * SM_W)
    value_blocks = v_soft[0].reshape(blocks, BLK * SM_W)
    send_keys = jnp.einsum(
        "rj,jc->rc", selection, key_blocks, preferred_element_type=jnp.bfloat16
    ).reshape(groups, BLK, SM_W)
    send_values = jnp.einsum(
        "rj,jc->rc", selection, value_blocks, preferred_element_type=jnp.bfloat16
    ).reshape(groups, BLK, SM_W)
    recv_keys, recv_values = (
        lax.all_to_all(send_keys, "files", split_axis=0, concat_axis=0, tiled=True),
        lax.all_to_all(send_values, "files", split_axis=0, concat_axis=0, tiled=True),
    )
    id_row = import_ids[0, 0]
    listed = jnp.arange(list_len) < import_counts[0, 0]
    owners = jnp.maximum(id_row, 0) // blocks
    imp_keys = jnp.take(recv_keys, owners, axis=0).reshape(list_len * BLK, SM_HEADS, SM_HD)
    key_valid = jnp.repeat(listed, BLK)
    queries = q_soft[0].reshape(tokens, SM_HEADS, SM_HD)
    own_q = q_soft[0].reshape(blocks, BLK, SM_HEADS, SM_HD)
    own_k = k_soft[0].reshape(blocks, BLK, SM_HEADS, SM_HD)
    own_v = v_soft[0].reshape(blocks, BLK, SM_HEADS, SM_HD)
    own_scores = (
        jnp.einsum("bqhd,bkhd->hbqk", own_q, own_k, preferred_element_type=jnp.float32) * scale
    )
    own_scores = own_scores.reshape(SM_HEADS, tokens, BLK)
    imp_scores = (
        jnp.einsum("qhd,khd->hqk", queries, imp_keys, preferred_element_type=jnp.float32) * scale
    )
    imp_scores = jnp.where(key_valid[None, None, :], imp_scores, -jnp.inf)
    top = jnp.maximum(jnp.max(own_scores, axis=-1), jnp.max(imp_scores, axis=-1))
    own_prob = jnp.exp(own_scores - top[..., None])
    imp_prob = jnp.exp(imp_scores - top[..., None])
    total = jnp.sum(own_prob, axis=-1) + jnp.sum(imp_prob, axis=-1)
    own_prob4 = own_prob.astype(jnp.bfloat16).reshape(SM_HEADS, blocks, BLK, BLK)
    own_num = jnp.einsum("hbqk,bkhd->bqhd", own_prob4, own_v, preferred_element_type=jnp.float32)
    own_num = own_num.reshape(tokens, SM_HEADS, SM_HD)
    imp_prob_b = imp_prob.astype(jnp.bfloat16)
    imp_values = jnp.take(recv_values, owners, axis=0).reshape(list_len * BLK, SM_HEADS, SM_HD)
    imp_num = jnp.einsum("hqk,khd->qhd", imp_prob_b, imp_values, preferred_element_type=jnp.float32)
    output = (own_num + imp_num) / total.T[..., None]
    return output.astype(jnp.bfloat16).reshape(1, tokens, SM_W)


def body(q_lin, k_lin, v_lin, q_soft, k_soft, v_soft, import_ids, import_counts):
    tokens = q_lin.shape[1]
    blocks = tokens // BLK
    lin_out = linear_layer(q_lin[0], k_lin[0], v_lin[0], tokens, blocks)
    soft_out = softmax_layer(q_soft, k_soft, v_soft, import_ids, import_counts, tokens, blocks)
    return (lin_out, soft_out)


def solution(mesh):
    placed = (
        P("files", "seq", None),
        P("files", "seq", None),
        P("files", "seq", None),
        P("files", "seq", None),
        P("files", "seq", None),
        P("files", "seq", None),
        P("files", "seq", None),
        P("files", "seq"),
    )
    return jax.shard_map(
        body,
        mesh=mesh,
        in_specs=placed,
        out_specs=(P("files", "seq", None), P("files", "seq", None)),
        check_vma=False,
    )
```

profile of v0, /device:TPU:24, one launch (start us, length us, event | category | flops | bytes accessed | tf_op | source)
XLA Modules:
  0.0 199.3 jit_solution(14333257221620104616)
XLA Ops:
  7.2 0.7 pad_clamp_fusion.2
  7.9 0.7 pad_clamp_fusion.1
  8.6 1.6 fusion.37
  10.4 1.0 fusion.38
  11.6 2.6 %gather_fusion.3 = f32[136,256,20]{1,2,0:T(8,128)} fusion(f32[256,20,16]{0,1,2:T(8,128)S(1)} %copy.174, s32[1024]{0:T(1024)S(1)} %pad_clamp_fusion.1), kind=kCustom, calls=%fused_computation.5 | custom fusion | bytes 5571104 | tf_op jit(solution)/shard_map/gather | solution.py:40
  14.2 2.6 %gather_fusion.2 = f32[136,256,20]{1,2,0:T(8,128)} fusion(f32[256,20,16]{0,1,2:T(8,128)S(1)} %copy.174, s32[1024]{0:T(1024)S(1)} %pad_clamp_fusion.2), kind=kCustom, calls=%fused_computation.4 | custom fusion | bytes 5571104 | tf_op jit(solution)/shard_map/gather | solution.py:40
  16.8 2.5 %gather_fusion = f32[136,256,20]{1,2,0:T(8,128)} fusion(f32[256,20,16]{0,1,2:T(8,128)S(1)} %copy.169, s32[1024]{0:T(1024)S(1)} %pad_clamp_fusion.2), kind=kCustom, calls=%fused_computation.2 | custom fusion | bytes 5571104 | tf_op jit(solution)/shard_map/gather | solution.py:40
  19.3 2.6 %gather_fusion.1 = f32[136,256,20]{1,2,0:T(8,128)} fusion(f32[256,20,16]{0,1,2:T(8,128)S(1)} %copy.169, s32[1024]{0:T(1024)S(1)} %pad_clamp_fusion.1), kind=kCustom, calls=%fused_computation.3 | custom fusion | bytes 5571104 | tf_op jit(solution)/shard_map/gather | solution.py:40
  21.9 0.7 mul.81
  22.6 1.3 copy.178
  23.9 3.5 %reshape.266 = bf16[2,128,20,128]{3,2,1,0:T(8,128)(2,1)} reshape(bf16[1,256,2560]{2,1,0:T(8,128)(2,1)} %param.24) | data formatting | bytes 2621440 | tf_op jit(solution)/shard_map/reshape;squeeze | solution.py:70
  27.4 4.1 %multiply_bitcast_fusion = f32[256,20,136]{0,1,2:T(8,128)} fusion(f32[136,256,20]{1,2,0:T(8,128)} %gather_fusion.2, f32[136,256,20]{1,2,0:T(8,128)S(1)} %copy-done.1), kind=kLoop, calls=%fused_computation.10 | loop fusion | flops 696320 | bytes 8355840 | tf_op jit(solution)/shard_map/mul | solution.py:40
  31.6 5.2 %reshape.265 = f32[2,128,20,136]{1,0,2,3:T(2,128)} reshape(f32[256,20,136]{0,1,2:T(8,128)} %multiply_bitcast_fusion) | data formatting | bytes 5570560 | tf_op jit(solution)/shard_map/mul | solution.py:40
  36.8 4.1 %multiply_bitcast_fusion.1 = f32[256,20,136]{0,1,2:T(8,128)} fusion(f32[136,256,20]{1,2,0:T(8,128)S(1)} %copy-done, f32[136,256,20]{1,2,0:T(8,128)} %gather_fusion.1), kind=kLoop, calls=%fused_computation.11 | loop fusion | flops 696320 | bytes 8355840 | tf_op jit(solution)/shard_map/mul | solution.py:40
  40.9 5.1 %reshape.264 = f32[2,128,20,136]{1,0,2,3:T(2,128)} reshape(f32[256,20,136]{0,1,2:T(8,128)} %multiply_bitcast_fusion.1) | data formatting | bytes 5570560 | tf_op jit(solution)/shard_map/mul | solution.py:40
  46.0 5.1 %fusion.2 = (bf16[2,128,20,136]{1,3,2,0:T(8,128)(2,1)S(1)}, bf16[2,128,20,136]{1,3,2,0:T(8,128)(2,1)}) fusion(f32[2,128,20,136]{1,0,2,3:T(2,128)} %reshape.265, f32[136]{0:T(256)S(1)} %copy-done.14, f32[2,128,20,136]{1,0,2,3:T(2,128)} %reshape.264), kind=kLoop, calls=%fused_computation.15 | loop fusion | flops 2785280 | bytes 8356384 | tf_op jit(solution)/shard_map/convert.2
  51.0 3.9 %fusion.58 = (f32[20,153,128]{2,1,0:T(8,128)}, f32[2,20,153,128]{3,2,1,0:T(8,128)}) fusion(bf16[2,128,20,128]{3,2,1,0:T(8,128)(2,1)S(1)} %copy-done.2, bf16[2,128,20,136]{1,3,2,0:T(8,128)(2,1)S(1)} %get-tuple-element.73, bf16[2,128,20,16]{1,3,2,0:T(8,128)(2,1)S(1)} %copy.178, bf16[153]{0:T(256)(128)(2,1)S(1)} %pad.5.clone), kind=kOutput, calls=%fused_computation.106 | convolution fusion | flops 205632000 | bytes 7567666 | tf_op jit(solution)/shard_map/bkhf,bkhd->bhfd/dot_general | solution.py:81
  56.4 3.7 %all-to-all-start = ((s32[8,1,1]{2,1,0:T(1,128)}), s32[8,1,1]{2,1,0:T(1,128)S(1)}, u32[]{:S(2)}, u32[]{:S(2)}) async-start(s32[8,1,1]{2,1,0:T(1,128)} %copy.189), calls=%async_computation | async-start | bytes 8192 | tf_op jit(solution)/shard_map/all_to_all | solution.py:105
  60.2 2.1 %reshape_squeeze.27 = bf16[2,163840]{1,0:T(2,128)(2,1)} reshape(bf16[1,256,1280]{2,1,0:T(8,128)(2,1)} %param.27) | data formatting | bytes 1310720 | tf_op jit(solution)/shard_map/reshape;squeeze | solution.py:117
  62.2 2.5 %all-to-all-done = s32[8,1,1]{2,1,0:T(1,128)S(1)} async-done(((s32[8,1,1]{2,1,0:T(1,128)}), s32[8,1,1]{2,1,0:T(1,128)S(1)}, u32[]{:S(2)}, u32[]{:S(2)}) %all-to-all-start) | async-done | bytes 64 | tf_op jit(solution)/shard_map/all_to_all | solution.py:105
  65.0 2.4 %fusion.43 = bf16[8,128,1280]{2,0,1:T(8,128)(2,1)S(1)} fusion(bf16[128,1280,2]{1,2,0:T(2,128)(2,1)} %bitcast.119, s32[8]{0:T(128)S(1)} %reduce.3, s32[2]{0:T(128)S(1)} %iota_add_fusion), kind=kOutput, calls=%fused_computation.78 | convolution fusion | flops 5242896 | bytes 3276840 | tf_op jit(solution)/shard_map/rj,jc->rc/dot_general | solution.py:121
  67.4 1.9 copy.199
  69.3 4.6 %all-to-all-start.2 = ((bf16[8,128,1280]{2,1,0:T(8,128)(2,1)}), bf16[8,128,1280]{2,1,0:T(8,128)(2,1)}, u32[]{:S(2)}, u32[]{:S(2)}) async-start(bf16[8,128,1280]{2,1,0:T(8,128)(2,1)} %copy.199), calls=%async_computation.2 | async-start | bytes 5242880 | tf_op jit(solution)/shard_map/all_to_all | solution.py:126
  73.9 2.2 %copy.192 = bf16[1,256,1280]{1,2,0:T(8,128)(2,1)} copy(bf16[1,256,1280]{2,1,0:T(8,128)(2,1)} %param.25) | data formatting | bytes 1310720 | tf_op args[3]
  76.0 2.3 %reshape.268 = bf16[2,128,10,128]{3,2,1,0:T(8,128)(2,1)} reshape(bf16[1,256,1280]{2,1,0:T(8,128)(2,1)} %param.25) | data formatting | bytes 1310720 | tf_op jit(solution)/shard_map/reshape;squeeze | solution.py:134
  78.4 2.1 %reshape_squeeze.24 = bf16[2,163840]{1,0:T(2,128)(2,1)} reshape(bf16[1,256,1280]{2,1,0:T(8,128)(2,1)} %param.26) | data formatting | bytes 1310720 | tf_op jit(solution)/shard_map/reshape;squeeze | solution.py:116
  80.5 2.3 %reshape.269 = bf16[2,128,10,128]{3,2,1,0:T(8,128)(2,1)} reshape(bf16[1,256,1280]{2,1,0:T(8,128)(2,1)} %param.26) | data formatting | bytes 1310720 | tf_op jit(solution)/shard_map/reshape;squeeze | solution.py:135
  82.8 2.2 %reshape.271 = bf16[2,128,10,128]{3,2,1,0:T(8,128)(2,1)} reshape(bf16[1,256,1280]{2,1,0:T(8,128)(2,1)} %param.27) | data formatting | bytes 1310720 | tf_op jit(solution)/shard_map/reshape;squeeze | solution.py:136
  85.1 0.7 copy.173
  85.8 2.3 %fusion.45 = bf16[8,128,1280]{2,0,1:T(8,128)(2,1)S(1)} fusion(bf16[128,1280,2]{1,2,0:T(2,128)(2,1)} %bitcast.118, s32[8]{0:T(128)S(1)} %reduce.3, s32[2]{0:T(128)S(1)} %iota_add_fusion), kind=kOutput, calls=%fused_computation.80 | convolution fusion | flops 5242896 | bytes 3276840 | tf_op jit(solution)/shard_map/rj,jc->rc/dot_general | solution.py:118
  88.1 1.9 copy.190
  90.1 15.9 %all-to-all-done.2 = bf16[8,128,1280]{2,1,0:T(8,128)(2,1)} async-done(((bf16[8,128,1280]{2,1,0:T(8,128)(2,1)}), bf16[8,128,1280]{2,1,0:T(8,128)(2,1)}, u32[]{:S(2)}, u32[]{:S(2)}) %all-to-all-start.2) | async-done | bytes 2621472 | tf_op jit(solution)/shard_map/all_to_all | solution.py:126
  106.0 4.4 %all-to-all-start.1 = ((bf16[8,128,1280]{2,1,0:T(8,128)(2,1)}), bf16[8,128,1280]{2,1,0:T(8,128)(2,1)}, u32[]{:S(2)}, u32[]{:S(2)}) async-start(bf16[8,128,1280]{2,1,0:T(8,128)(2,1)} %copy.190), calls=%async_computation.1 | async-start | bytes 5242880 | tf_op jit(solution)/shard_map/all_to_all | solution.py:125
  110.4 3.4 %fusion.59 = (f32[10,2,128]{2,1,0:T(2,128)S(1)}, f32[10,2,128,128]{2,3,1,0:T(8,128)}) fusion(bf16[2,128,10,128]{3,2,1,0:T(8,128)(2,1)} %reshape.269, bf16[2,128,10,128]{3,2,1,0:T(8,128)(2,1)} %reshape.268), kind=kOutput, calls=%fused_computation.107 | convolution fusion | flops 84538880 | bytes 2631680 | tf_op jit(solution)/shard_map/bqhd,bkhd->hbqk/dot_general | solution.py:138
  113.8 2.3 %convert_reduce_fusion = (f32[2,20,153]{2,1,0:T(8,128)S(1)}, f32[20,153]{1,0:T(8,128)S(1)}) fusion(bf16[2,128,20,136]{1,3,2,0:T(8,128)(2,1)S(1)} %get-tuple-element.73, bf16[2,128,20,16]{1,3,2,0:T(8,128)(2,1)S(1)} %copy.178, bf16[153]{0:T(256)(128)(2,1)S(1)} %pad.5.clone), kind=kLoop, calls=%fused_computation.8 | loop fusion | flops 6257700 | bytes 1593506 | tf_op jit(solution)/shard_map/reduce_sum | solution.py:82
  116.1 15.5 %all-gather.2 = f32[4,20,153]{2,1,0:T(8,128)} all-gather(f32[1,20,153]{2,1,0:T(8,128)S(1)} %bitcast.123), channel_id=3, replica_groups=mesh['seq'=4,'files'=8] {'seq'}, dimensions={0}, use_global_device_ids=true | all-gather | bytes 61200 | tf_op jit(solution)/shard_map/all_gather | solution.py:25
  131.7 2.4 %multiply_reduce_fusion = (f32[2,20,128]{2,1,0:T(8,128)}, f32[2,20,128,128]{2,3,1,0:T(8,128)S(1)}) fusion(f32[128,128]{0,1:T(8,128)S(1)} %fusion.36, bf16[2,128,20,136]{1,3,2,0:T(8,128)(2,1)S(1)} %get-tuple-element.73, bf16[2,128,20,16]{1,3,2,0:T(8,128)(2,1)S(1)} %copy.178, bf16[153]{0:T(256)(128)(2,1)S(1)} %pad.5.clone, ...), kind=kOutput, calls=%fused_computation.25 | convolution fusion | flops 211246080 | bytes 5820722 | tf_op jit(solution)/shard_map/bqhf,bkhf->bhqk/dot_general | solution.py:72
  134.1 2.1 %fusion.11 = f32[2,20,153,128]{3,2,1,0:T(8,128)} fusion(f32[2,20,153,128]{3,2,1,0:T(8,128)S(1)} %copy-done.3), kind=kOutput, calls=%fused_computation.29 | output fusion | flops 783360 | bytes 4771840 | tf_op jit(solution)/shard_map/jit(cumsum)/reduce_window_sum | solution.py:47
  136.2 2.1 %fusion.18 = f32[2,20,128,128]{3,2,1,0:T(8,128)} fusion(f32[2,20,128,128]{2,3,1,0:T(8,128)S(1)} %get-tuple-element.82, f32[128,128]{0,1:T(8,128)S(1)} %fusion.36, bf16[2,128,20,128]{3,2,1,0:T(8,128)(2,1)S(1)} %copy-done.2), kind=kOutput, calls=%fused_computation.40 | convolution fusion | flops 169082880 | bytes 6619136 | tf_op jit(solution)/shard_map/bhqk,bkhd->bqhd/dot_general | solution.py:75
  138.3 2.3 %gather_fusion.5 = bf16[2,128,1280]{2,1,0:T(8,128)(2,1)S(1)} fusion(bf16[8,128,1280]{2,1,0:T(8,128)(2,1)} %all-to-all-done.2, s32[1024]{0:T(1024)S(1)} %pad_clamp_fusion), kind=kCustom, calls=%fused_computation.1.clone | custom fusion | bytes 1310728 | tf_op jit(solution)/shard_map/jit(_take)/gather | solution.py:153
  140.6 2.0 %all-to-all-done.1 = bf16[8,128,1280]{2,1,0:T(8,128)(2,1)} async-done(((bf16[8,128,1280]{2,1,0:T(8,128)(2,1)}), bf16[8,128,1280]{2,1,0:T(8,128)(2,1)}, u32[]{:S(2)}, u32[]{:S(2)}) %all-to-all-start.1) | async-done | bytes 2621472 | tf_op jit(solution)/shard_map/all_to_all | solution.py:125
  142.7 2.3 %gather_fusion.4 = bf16[2,128,1280]{2,1,0:T(8,128)(2,1)S(1)} fusion(bf16[8,128,1280]{2,1,0:T(8,128)(2,1)} %all-to-all-done.1, s32[1024]{0:T(1024)S(1)} %pad_clamp_fusion), kind=kCustom, calls=%fused_computation.clone | custom fusion | bytes 1310728 | tf_op jit(solution)/shard_map/jit(_take)/gather | solution.py:131
  145.2 0.9 copy.200
  146.1 1.3 reshape.200
  147.4 1.4 reshape.270
  148.9 1.8 bitcast_reduce_fusion
  150.7 1.6 fusion.24
  152.3 1.6 convolution_bitcast_fusion.1
  153.9 1.1 copy.198
  155.0 2.9 %copy.202 = f32[256,10,128]{0,2,1:T(8,128)} copy(f32[256,10,128]{2,0,1:T(8,128)} %bitcast.116) | data formatting | bytes 2621440 | tf_op jit(solution)/shard_map/reshape | solution.py:151
  159.3 1.7 fusion.16
  161.0 2.2 %copy.204 = bf16[1,256,1280]{2,1,0:T(8,128)(2,1)} copy(bf16[1,256,1280]{1,2,0:T(8,128)(2,1)} %bitcast.122) | data formatting | bytes 1310720
  163.1 11.1 %all-gather.5.cloned.1.call-done = f32[80,153,128]{2,1,0:T(8,128)} async-done(((f32[20,153,128]{2,1,0:T(8,128)}), f32[80,153,128]{2,1,0:T(8,128)}) %all-gather.5.cloned.1.call-update) | async-done | bytes 6266896 | tf_op jit(solution)/shard_map/all_gather | solution.py:25
  174.4 8.2 %while.12 = (s32[]{:T(128)}, f32[20,153,128]{2,1,0:T(8,128)S(1)}, f32[20,153]{1,0:T(8,128)S(1)}, s32[]{:T(128)}, f32[4,20,153,128]{3,2,1,0:T(8,128)}, /*index=5*...) while((s32[]{:T(128)}, f32[20,153,128]{2,1,0:T(8,128)S(1)}, f32[20,153]{1,0:T(8,128)S(1)}, s32[]{:T(128)}, ...), condition=%wide.region_3.4_spmd, body=%wide.region_2.3_spmd.sunk | while | flops 394745 | bytes 4737023 | solution.py:33
  174.4 0.9 bitcast_add_fusion.7
  175.3 1.8 bitcast_add_fusion.6
  177.1 0.7 bitcast_add_fusion.7
  177.9 1.8 bitcast_add_fusion.6
  179.8 0.7 bitcast_add_fusion.7
  180.5 1.8 bitcast_add_fusion.6
  182.7 1.5 fusion.39
  184.6 5.4 %fusion.6 = bf16[2,128,20,128]{3,1,2,0:T(8,128)(2,1)S(1)} fusion(f32[2,20,128,128]{3,2,1,0:T(8,128)} %fusion.18, f32[2,20,153,128]{3,2,1,0:T(8,128)S(1)} %copy-done.4, f32[20,153,128]{2,1,0:T(8,128)S(1)} %get-tuple-element.37, f32[2,128,20]{1,2,0:T(8,128)S(1)} %fusion.42, bf16[2,128,20,136]{1,3,2,0:T(8,128)(2,1)S(1)} %copy-done.7, ...), kind=kOutput, calls=%fused_computation.23 | convolution fusion | flops 1210690560 | bytes 10209586 | tf_op jit(solution)/shard_map/bqhf,bhfd->bqhd/dot_general | solution.py:89
  190.0 0.9 copy.220
  190.9 1.6 reshape.267
  (62 shorter events, 3.7 us)
Async XLA Ops:
  7.2 167.1 %all-gather.5.cloned.1.call-start = ((), (), s32[]{:S(2)}) async-start(), calls=%async_computation.3 | async-start | bytes 8192000 | tf_op jit(solution)/shard_map/all_gather | solution.py:25
  21.9 5.5 %copy-start.1 = (f32[136,256,20]{1,2,0:T(8,128)S(1)}, f32[136,256,20]{1,2,0:T(8,128)}, u32[]{:S(2)}) copy-start(f32[136,256,20]{1,2,0:T(8,128)} %gather_fusion.3) | copy-start | bytes 8355844
  31.6 5.2 %copy-start = (f32[136,256,20]{1,2,0:T(8,128)S(1)}, f32[136,256,20]{1,2,0:T(8,128)}, u32[]{:S(2)}) copy-start(f32[136,256,20]{1,2,0:T(8,128)} %gather_fusion) | copy-start | bytes 8355844
  40.9 5.1 %copy-start.14 = (f32[136]{0:T(256)S(1)}, f32[136]{0:T(256)}, u32[]{:S(2)}) copy-start(f32[136]{0:T(256)} %constant.106.clone) | copy-start | bytes 1636
  46.0 5.1 %copy-start.2 = (bf16[2,128,20,128]{3,2,1,0:T(8,128)(2,1)S(1)}, bf16[2,128,20,128]{3,2,1,0:T(8,128)(2,1)}, u32[]{:S(2)}) copy-start(bf16[2,128,20,128]{3,2,1,0:T(8,128)(2,1)} %reshape.266) | copy-start | bytes 3932164
  51.0 4.6 %copy-start.15 = (s32[1,1,2]{2,1,0:T(1,128)S(1)}, s32[1,1,2]{2,1,0:T(1,128)}, u32[]{:S(2)}) copy-start(s32[1,1,2]{2,1,0:T(1,128)} %param.28) | copy-start | bytes 28
  56.4 8.3 %all-to-all-start = ((s32[8,1,1]{2,1,0:T(1,128)}), s32[8,1,1]{2,1,0:T(1,128)S(1)}, u32[]{:S(2)}, u32[]{:S(2)}) async-start(s32[8,1,1]{2,1,0:T(1,128)} %copy.189), calls=%async_computation | async-start | bytes 8192 | tf_op jit(solution)/shard_map/all_to_all | solution.py:105
  69.3 36.7 %all-to-all-start.2 = ((bf16[8,128,1280]{2,1,0:T(8,128)(2,1)}), bf16[8,128,1280]{2,1,0:T(8,128)(2,1)}, u32[]{:S(2)}, u32[]{:S(2)}) async-start(bf16[8,128,1280]{2,1,0:T(8,128)(2,1)} %copy.199), calls=%async_computation.2 | async-start | bytes 5242880 | tf_op jit(solution)/shard_map/all_to_all | solution.py:126
  78.4 6.7 %copy-start.9 = (bf16[1,256,320]{1,2,0:T(8,128)(2,1)S(1)}, bf16[1,256,320]{1,2,0:T(8,128)(2,1)}, u32[]{:S(2)}) copy-start(bf16[1,256,320]{1,2,0:T(8,128)(2,1)} %get-tuple-element.71) | copy-start | bytes 491524
  106.0 36.7 %all-to-all-start.1 = ((bf16[8,128,1280]{2,1,0:T(8,128)(2,1)}), bf16[8,128,1280]{2,1,0:T(8,128)(2,1)}, u32[]{:S(2)}, u32[]{:S(2)}) async-start(bf16[8,128,1280]{2,1,0:T(8,128)(2,1)} %copy.190), calls=%async_computation.1 | async-start | bytes 5242880 | tf_op jit(solution)/shard_map/all_to_all | solution.py:125
  110.4 21.3 %copy-start.6 = (bf16[2,128,20,136]{1,3,2,0:T(8,128)(2,1)S(1)}, bf16[2,128,20,136]{1,3,2,0:T(8,128)(2,1)}, u32[]{:S(2)}) copy-start(bf16[2,128,20,136]{1,3,2,0:T(8,128)(2,1)} %get-tuple-element.74) | copy-start | bytes 4177924
  110.4 21.3 %copy-start.11 = (bf16[2,128,20,16]{1,3,2,0:T(8,128)(2,1)S(1)}, bf16[2,128,20,16]{1,3,2,0:T(8,128)(2,1)}, u32[]{:S(2)}) copy-start(bf16[2,128,20,16]{1,3,2,0:T(8,128)(2,1)} %copy.173) | copy-start | bytes 491524
  131.7 2.4 %copy-start.3 = (f32[2,20,153,128]{3,2,1,0:T(8,128)S(1)}, f32[2,20,153,128]{3,2,1,0:T(8,128)}, u32[]{:S(2)}) copy-start(f32[2,20,153,128]{3,2,1,0:T(8,128)} %get-tuple-element.80) | copy-start | bytes 9400324
  145.2 3.7 %copy-start.5 = (bf16[1,256,1280]{1,2,0:T(8,128)(2,1)S(1)}, bf16[1,256,1280]{1,2,0:T(8,128)(2,1)}, u32[]{:S(2)}) copy-start(bf16[1,256,1280]{1,2,0:T(8,128)(2,1)} %copy.192) | copy-start | bytes 1966084
  155.0 3.6 %copy-start.10 = (bf16[256,10,128]{0,2,1:T(8,128)(2,1)S(1)}, bf16[256,10,128]{0,2,1:T(8,128)(2,1)}, u32[]{:S(2)}) copy-start(bf16[256,10,128]{0,2,1:T(8,128)(2,1)} %reshape.200) | copy-start | bytes 1966084
  158.0 1.3 copy-start.8
  174.4 8.3 %copy-start.7 = (bf16[2,128,20,136]{1,3,2,0:T(8,128)(2,1)S(1)}, bf16[2,128,20,136]{1,3,2,0:T(8,128)(2,1)}, u32[]{:S(2)}) copy-start(bf16[2,128,20,136]{1,3,2,0:T(8,128)(2,1)} %get-tuple-element.74) | copy-start | bytes 4177924
  174.4 8.3 %copy-start.12 = (bf16[2,128,20,16]{1,3,2,0:T(8,128)(2,1)S(1)}, bf16[2,128,20,16]{1,3,2,0:T(8,128)(2,1)}, u32[]{:S(2)}) copy-start(bf16[2,128,20,16]{1,3,2,0:T(8,128)(2,1)} %copy.173) | copy-start | bytes 491524
  182.6 1.7 copy-start.13
  182.6 1.9 copy-start.4
Sparse Core Ops, SparseCore 0:
  55.1 119.0 all-gather.4
where the time goes:
time: 201 us; the launch traced here: 199 us
  local copies, waits for them, and re-layouts  63.4 us (32%)
  other arithmetic  32.3 us (16%)
  waiting for transfers between devices  31.5 us (16%)
  matrix products  28.5 us (14%)
  blocking collectives  15.5 us (8%)
  between operations  15 us (7%)
  starting transfers between devices  12.8 us (6%)
    all_to_all x1, waiting for transfers between devices, softmax_layer(): lax.all_to_all(send_values, 'files', split_axis=0, concat_axis=0, tiled=T...  15.9 us
    all_gather x1, blocking collectives, entering(): gathered = jax.tree.map(lambda a: lax.all_gather(a, axis), part)  15.5 us
    all_gather x1, waiting for transfers between devices, entering(): gathered = jax.tree.map(lambda a: lax.all_gather(a, axis), part)  11.1 us
    gather x4, local copies, waits for them, and re-layouts, feature_map(): quadratic = inputs[..., rows] * inputs[..., cols] * factor  10.3 us
    mul x2, local copies, waits for them, and re-layouts, feature_map(): quadratic = inputs[..., rows] * inputs[..., cols] * factor  10.3 us
    mul x2, other arithmetic, feature_map(): quadratic = inputs[..., rows] * inputs[..., cols] * factor  8.25 us
    unnamed x40, local copies, waits for them, and re-layouts  7.88 us
    add x6, other arithmetic, add_pairs(): return (earlier[0] + later[0], earlier[1] + later[1])  7.86 us
  transfers between devices with their start and end apart: 4, of which 4 were waited for; matrix products, arithmetic and copies ran while one was open for 29% of the time, Pallas kernels for 0%

commit v1 on v0

v1 whole, which is shorter than its diff:
```python
import functools
import math

import jax
import jax.numpy as jnp
import numpy as np
from jax import lax
from jax.experimental import pallas as pl
from jax.experimental.pallas import tpu as pltpu
from jax.sharding import PartitionSpec as P

FEAT = 16
FEATS = 153
FPAD = 160
HD = 128
SM_HD = 128
BLK = 128
ROWS = 16
GROUP = 4
MESH = pl.DeviceIdType.MESH
F32 = jnp.float32
BF16 = jnp.bfloat16


def selectors():
    rows, cols = np.triu_indices(FEAT)
    lanes = np.arange(128) % FEAT
    first = np.zeros((FPAD, 128), np.float32)
    second = np.zeros((FPAD, 128), np.float32)
    second_q = np.zeros((FPAD, 128), np.float32)
    for i in range(FEAT):
        first[1 + i] = 0.5 * (lanes == i)
    for f, (i, j) in enumerate(zip(rows, cols)):
        first[1 + FEAT + f] = 0.5 * (lanes == i)
        second[1 + FEAT + f] = 0.5 * (lanes == j)
        second_q[1 + FEAT + f] = (0.25 if i == j else 0.5) * (lanes == j)
    for_k = np.concatenate([first, second])
    gap = np.zeros((256 - FPAD, 128), np.float32)
    for_q = np.concatenate([first, gap, second_q, gap])
    return for_k, for_q


def nt(a, b):
    return lax.dot_general(a, b, (((1,), (1,)), ((), ())), preferred_element_type=F32)


def nn(a, b):
    return lax.dot_general(a, b, (((1,), (0,)), ((), ())), preferred_element_type=F32)


def kernel(
    dims,
    q_ref, k_ref, v_ref, qs_ref, ks_hbm, vs_hbm, ids_ref, bias_ref, ek_ref, eq_ref,
    lin_ref, soft_ref,
    kv, pieces, outgoing, imp, tbl, tbl_s, qp, kp,
    local, s_send, s_recv, n_local, n_send, n_recv, own_num, own_max, own_sum,
    load_sem, ids_send, ids_recv, p1_send, p1_recv, p2_send, p2_recv,
    st_send, st_recv, nm_send, nm_recv, tbl_sem,
):
    n, nz, heads, sm_heads, blocks, maxb, kvs, cols = dims
    tokens = blocks * BLK
    me = lax.axis_index("files")
    z = lax.axis_index("seq")
    has_prev = z > 0
    has_next = z < nz - 1

    def peer(off):
        return lax.rem(me + off, n)

    def piece(p):
        if kvs == 2:
            col = lax.rem(p, n * ROWS // BLK)
            row = p // (n * ROWS // BLK)
            at_kv = pl.ds(0, 2)
        else:
            halves = n * ROWS // BLK // 2
            col = lax.rem(p, halves)
            row = p // (2 * halves)
            at_kv = pl.ds(lax.rem(p // halves, 2), 1)
        return at_kv, pl.ds(pl.multiple_of(row * ROWS, ROWS), ROWS), pl.ds(
            pl.multiple_of(col * cols, 128), cols
        )

    load_k = pltpu.make_async_copy(ks_hbm, kv.at[:, 0], load_sem.at[0])
    load_v = pltpu.make_async_copy(vs_hbm, kv.at[:, 1], load_sem.at[1])
    load_k.start()
    load_v.start()

    barrier = pltpu.get_barrier_semaphore()
    for off in range(1, n):
        pl.semaphore_signal(barrier, inc=1, device_id={"files": peer(off)}, device_id_type=MESH)

    @pl.when(has_prev)
    def _():
        pl.semaphore_signal(barrier, inc=1, device_id={"seq": z - 1}, device_id_type=MESH)

    @pl.when(has_next)
    def _():
        pl.semaphore_signal(barrier, inc=1, device_id={"seq": z + 1}, device_id_type=MESH)

    neighbours = (z + nz - 1) // nz + (2 * nz - 2 - z) // nz
    pl.semaphore_wait(barrier, n - 1 + neighbours)

    id_copies = []
    for off in range(1, n):
        c = pltpu.make_async_remote_copy(
            src_ref=ids_ref, dst_ref=tbl.at[me], send_sem=ids_send.at[off], recv_sem=ids_recv.at[off],
            device_id={"files": peer(off)}, device_id_type=MESH)
        c.start()
        id_copies.append(c)
    tbl[me] = ids_ref[...]
    load_k.wait()
    load_v.wait()
    first = []
    for off in range(1, n):
        to = peer(off)
        at_kv, at_row, at_col = piece(to)
        c = pltpu.make_async_remote_copy(
            src_ref=kv.at[:, at_kv, at_row, at_col], dst_ref=pieces.at[pl.ds(me * blocks, blocks)],
            send_sem=p1_send.at[off], recv_sem=p1_recv.at[off],
            device_id={"files": to}, device_id_type=MESH)
        c.start()
        first.append(c)
    at_kv, at_row, at_col = piece(me)
    mine = pltpu.make_async_copy(
        kv.at[:, at_kv, at_row, at_col], pieces.at[pl.ds(me * blocks, blocks)], load_sem.at[2])
    mine.start()

    lanes_in = heads * FEAT
    qp[...] = jnp.zeros_like(qp)
    kp[...] = jnp.zeros_like(kp)
    qp[:, :lanes_in] = q_ref[...]
    kp[:, :lanes_in] = k_ref[...]

    def head_tile(ref, h):
        lane = lax.broadcasted_iota(jnp.int32, (tokens, 128), 1)
        start = pl.multiple_of((h // 8) * 128, 128)
        tile = ref[:, pl.ds(start, 128)]
        low = lax.rem(h, 8) * FEAT
        inside = (lane >= low) & (lane < low + FEAT)
        return tile, jnp.where(inside, tile, jnp.zeros_like(tile))

    def lane_is(h, rows):
        return lax.broadcasted_iota(jnp.int32, (rows, 128), 1) == h

    def columns(h):
        return pl.ds(pl.multiple_of(h * HD, HD), HD)

    n_local[...] = jnp.zeros_like(n_local)

    def state_of(h):
        _, km = head_tile(kp, h)
        both = nt(ek_ref[...], km)
        row = lax.broadcasted_iota(jnp.int32, (FPAD, tokens), 0)
        feat = jnp.where(row == 0, 1.0, both[:FPAD]) * jnp.where(row < 1 + FEAT, 1.0, both[FPAD:])
        ones = jnp.where(lane_is(h, tokens), 1.0, 0.0).astype(BF16)
        right = jnp.concatenate([v_ref[:, columns(h)], ones], axis=1)
        made = nn(feat.astype(BF16), right)
        local[h] = made[:, :HD]
        return made[:, HD:]

    def states(i, carry):
        n_local[...] += state_of(2 * i) + state_of(2 * i + 1)
        return carry

    lax.fori_loop(0, heads // 2, states, 0)

    groups = heads // GROUP

    def norm_copy():
        return pltpu.make_async_remote_copy(
            src_ref=n_send, dst_ref=n_recv, send_sem=nm_send, recv_sem=nm_recv,
            device_id={"seq": lax.rem(z + 1, nz)}, device_id_type=MESH)

    def state_copy(g):
        at = pl.ds(g * GROUP, GROUP)
        return pltpu.make_async_remote_copy(
            src_ref=s_send.at[at], dst_ref=s_recv.at[at], send_sem=st_send.at[g], recv_sem=st_recv.at[g],
            device_id={"seq": lax.rem(z + 1, nz)}, device_id_type=MESH)

    @pl.when(z == 0)
    def _():
        n_recv[...] = jnp.zeros_like(n_recv)
        s_recv[...] = jnp.zeros_like(s_recv)

    @pl.when(has_prev)
    def _():
        norm_copy().wait_recv()

    @pl.when(has_next)
    def _():
        n_send[...] = n_recv[...] + n_local[...]
        norm_copy().start()

    def pass_on(g):
        at = pl.ds(g * GROUP, GROUP)

        @pl.when(has_prev)
        def _():
            state_copy(g).wait_recv()

        @pl.when(has_next)
        def _():
            s_send[at] = (s_recv[at].astype(F32) + local[at]).astype(BF16)
            state_copy(g).start()

    def lin_head(h, norms):
        _, qm = head_tile(qp, h)
        k_tile, _ = head_tile(kp, h)
        s = nt(qm, k_tile) * 0.25
        t_at = lax.broadcasted_iota(jnp.int32, (tokens, tokens), 0)
        s_at = lax.broadcasted_iota(jnp.int32, (tokens, tokens), 1)
        w = jnp.where(s_at <= t_at, 1.0 + s * (1.0 + 0.5 * s), 0.0)
        num = nn(w.astype(BF16), v_ref[:, columns(h)])
        both = nt(qm, eq_ref[...])
        lane = lax.broadcasted_iota(jnp.int32, (tokens, 256), 1)
        feat = jnp.where(lane == 0, 1.0, both[:, :256]) * jnp.where(lane < 1 + FEAT, 1.0, both[:, 256:])
        which = lane_is(h, FPAD) | lane_is(h + 64, FPAD)
        right = jnp.concatenate([s_recv[h], jnp.where(which, norms, jnp.zeros_like(norms))], axis=1)
        far = nn(feat[:, :FPAD].astype(BF16), right)
        den = jnp.sum(w, axis=1, keepdims=True) + jnp.sum(far[:, HD:], axis=1, keepdims=True)
        lin_ref[:, columns(h)] = ((num + far[:, :HD]) / den).astype(BF16)

    def lin_group(g):
        total = n_recv[...]
        high = total.astype(BF16)
        low = (total - high.astype(F32)).astype(BF16)
        norms = jnp.where(
            lax.broadcasted_iota(jnp.int32, (FPAD, 128), 1) < 64,
            high.astype(F32), pltpu.roll(low.astype(F32), 64, 1)).astype(BF16)

        def two(i, carry):
            lin_head(g * GROUP + 2 * i, norms)
            lin_head(g * GROUP + 2 * i + 1, norms)
            return carry

        lax.fori_loop(0, GROUP // 2, two, 0)

    scale = 1.0 / math.sqrt(SM_HD)

    def own_part(h, carry):
        at = columns(h)
        for b in range(blocks):
            rows = pl.ds(b * BLK, BLK)
            s = nt(qs_ref[rows, at], kv[b, 0, :, at]) * scale
            top = jnp.max(s, axis=1, keepdims=True)
            p = jnp.exp(s - top)
            own_max[h, rows] = top
            own_sum[h, rows] = jnp.sum(p, axis=1, keepdims=True)
            own_num[rows, at] = nn(p.astype(BF16), kv[b, 1, :, at])
        return carry

    def imported_part(h, carry):
        at = columns(h)
        keys = imp[:, 0, :, at].reshape(maxb * BLK, SM_HD)
        s = nt(qs_ref[:, at], keys) * scale + bias_ref[0:1, :]
        top = jnp.maximum(own_max[h], jnp.max(s, axis=1, keepdims=True))
        p = jnp.exp(s - top)
        before = jnp.exp(own_max[h] - top)
        total = own_sum[h] * before + jnp.sum(p, axis=1, keepdims=True)
        values = imp[:, 1, :, at].reshape(maxb * BLK, SM_HD)
        num = own_num[:, at] * before + nn(p.astype(BF16), values)
        soft_ref[:, at] = (num / total).astype(BF16)
        return carry

    second = []

    def exchange():
        for c in id_copies:
            c.wait_recv()
        to_smem = pltpu.make_async_copy(tbl, tbl_s, tbl_sem)
        to_smem.start()
        to_smem.wait()
        for c in first:
            c.wait_recv()
        mine.wait()
        at_kv, at_row, at_col = piece(me)
        for off in range(n):
            to = peer(off)
            for i in range(maxb):
                outgoing[off, i] = pieces[jnp.maximum(tbl_s[to, 0, i], 0)]
            there = imp.at[:, at_kv, at_row, at_col]
            if off == 0:
                c = pltpu.make_async_copy(outgoing.at[0], there, load_sem.at[3])
            else:
                c = pltpu.make_async_remote_copy(
                    src_ref=outgoing.at[off], dst_ref=there,
                    send_sem=p2_send.at[off], recv_sem=p2_recv.at[off],
                    device_id={"files": to}, device_id_type=MESH)
            c.start()
            second.append(c)

    pass_on(0)
    lax.fori_loop(0, sm_heads, own_part, 0)
    pass_on(1)
    exchange()
    for g in range(groups):
        if g >= 2:
            pass_on(g)
        lin_group(g)

    for c in second:
        if c is second[0]:
            c.wait()
        else:
            c.wait_recv()
    lax.fori_loop(0, sm_heads, imported_part, 0)

    for c in id_copies + first + second[1:]:
        c.wait_send()

    @pl.when(has_next)
    def _():
        norm_copy().wait_send()
        for g in range(groups):
            state_copy(g).wait_send()


def body(q_lin, k_lin, v_lin, q_soft, k_soft, v_soft, import_ids, import_counts):
    n, nz = lax.axis_size("files"), lax.axis_size("seq")
    tokens = q_lin.shape[1]
    blocks = tokens // BLK
    heads = q_lin.shape[2] // FEAT
    width, sm_w = v_lin.shape[2], q_soft.shape[2]
    sm_heads = sm_w // SM_HD
    maxb = import_ids.shape[2]
    col_parts = n * ROWS // BLK
    kvs = 2 if sm_w % (128 * col_parts) == 0 else 1
    cols = sm_w // col_parts if kvs == 2 else sm_w * 2 // col_parts
    lanes_in = -(-heads * FEAT // 128) * 128
    listed = jnp.arange(maxb) < import_counts[0, 0]
    ids = jnp.pad(jnp.where(listed, import_ids[0, 0], -1)[None], ((0, 7), (0, 128 - maxb)), constant_values=-1)
    bias = jnp.broadcast_to(
        jnp.repeat(jnp.where(listed, 0.0, -jnp.inf).astype(F32), BLK)[None], (8, maxb * BLK))
    for_k, for_q = selectors()
    dims = (n, nz, heads, sm_heads, blocks, maxb, kvs, cols)
    vmem = pl.BlockSpec(memory_space=pltpu.VMEM)
    hbm = pl.BlockSpec(memory_space=pl.ANY)
    dma = pltpu.SemaphoreType.DMA
    lin, soft = pl.pallas_call(
        functools.partial(kernel, dims),
        out_shape=(
            jax.ShapeDtypeStruct((tokens, width), BF16),
            jax.ShapeDtypeStruct((tokens, sm_w), BF16),
        ),
        in_specs=[vmem, vmem, vmem, vmem, hbm, hbm, vmem, vmem, vmem, vmem],
        out_specs=(vmem, vmem),
        scratch_shapes=[
            pltpu.VMEM((blocks, 2, BLK, sm_w), BF16),
            pltpu.VMEM((n * blocks, kvs, ROWS, cols), BF16),
            pltpu.VMEM((n, maxb, kvs, ROWS, cols), BF16),
            pltpu.VMEM((maxb, 2, BLK, sm_w), BF16),
            pltpu.VMEM((n, 8, 128), jnp.int32),
            pltpu.SMEM((n, 8, 128), jnp.int32),
            pltpu.VMEM((tokens, lanes_in), BF16),
            pltpu.VMEM((tokens, lanes_in), BF16),
            pltpu.VMEM((heads, FPAD, HD), F32),
            pltpu.VMEM((heads, FPAD, HD), BF16),
            pltpu.VMEM((heads, FPAD, HD), BF16),
            pltpu.VMEM((FPAD, HD), F32),
            pltpu.VMEM((FPAD, HD), F32),
            pltpu.VMEM((FPAD, HD), F32),
            pltpu.VMEM((tokens, sm_w), F32),
            pltpu.VMEM((sm_heads, tokens, 1), F32),
            pltpu.VMEM((sm_heads, tokens, 1), F32),
            dma((4,)), dma((n,)), dma((n,)), dma((n,)), dma((n,)), dma((n,)), dma((n,)),
            dma((heads // GROUP,)), dma((heads // GROUP,)), dma, dma, dma,
        ],
        compiler_params=pltpu.CompilerParams(
            collective_id=0, has_side_effects=True, vmem_limit_bytes=48 * 2**20),
    )(
        q_lin[0], k_lin[0], v_lin[0], q_soft[0],
        k_soft.reshape(blocks, BLK, sm_w), v_soft.reshape(blocks, BLK, sm_w),
        ids, bias, jnp.asarray(for_k, BF16), jnp.asarray(for_q, BF16),
    )
    return lin[None], soft[None]


def solution(mesh):
    row = P("files", "seq", None)
    return jax.shard_map(
        body,
        mesh=mesh,
        in_specs=(row,) * 7 + (P("files", "seq"),),
        out_specs=(row, row),
        check_vma=False,
    )
```

time: 201 us -> 64.4 us (0.32)
  local copies, waits for them, and re-layouts: 63.4 us -> 10.5 us
  Pallas kernels: 0 us -> 51.3 us
  other arithmetic: 32.3 us -> 0.66 us
  waiting for transfers between devices: 31.5 us -> 0 us
  matrix products: 28.5 us -> 0 us
  blocking collectives: 15.5 us -> 0 us
  between operations: 15 us -> 1.31 us
  starting transfers between devices: 12.8 us -> 0 us
    pallas_call x0 -> x1, Pallas kernels: none -> 51.3 us  [body(): pl.pallas_call(functools.partial(kernel, dims), out_shape=(jax.ShapeDtype...]
    dot_general x11 -> x0, matrix products: 28.5 us -> none  [the longest x1 5.42 us: linear_layer(): jnp.einsum('bqhf,bhfd->bqhd', feat_q32, state_in, precision=highest_preci...]
    all_to_all x3 -> x0, waiting for transfers between devices: 20.4 us -> none  [the longest x1 15.9 us: softmax_layer(): lax.all_to_all(send_values, 'files', split_axis=0, concat_axis=0, tiled=T...]
    all_gather x1 -> x0, blocking collectives: 15.5 us -> none  [entering(): gathered = jax.tree.map(lambda a: lax.all_gather(a, axis), part)]
    gather x6 -> x0, local copies, waits for them, and re-layouts: 15 us -> none  [the longest x4 10.3 us: feature_map(): quadratic = inputs[..., rows] * inputs[..., cols] * factor]
    another operation x6 -> x0, local copies, waits for them, and re-layouts: 14.6 us -> none  [the longest x1 3.53 us: linear_layer(): values = value_rows.reshape(blocks, BLK, HEADS, head_dim)]
    mul x8 -> x0, local copies, waits for them, and re-layouts: 13.4 us -> none  [the longest x2 10.3 us: feature_map(): quadratic = inputs[..., rows] * inputs[..., cols] * factor]
    all_to_all x3 -> x0, starting transfers between devices: 12.7 us -> none  [the longest x1 4.58 us: softmax_layer(): lax.all_to_all(send_values, 'files', split_axis=0, concat_axis=0, tiled=T...]
  transfers between devices with their start and end apart: 4 -> 0, of which waited for: 4 -> 0; matrix products, arithmetic and copies ran while one was open for 29% -> 0% of each run, Pallas kernels for 0% -> 0%
where the time goes in v1:
time: 64.4 us; the launch traced here: 63.8 us
  Pallas kernels  51.3 us (80%)
  local copies, waits for them, and re-layouts  10.5 us (16%)
  between operations  1.31 us (2%)
  other arithmetic  0.66 us (1%)
    pallas_call x1, Pallas kernels, body(): pl.pallas_call(functools.partial(kernel, dims), out_shape=(jax.ShapeDtype...  51.3 us
    unnamed x16, local copies, waits for them, and re-layouts  10.4 us

profile of v1, /device:TPU:24, one launch (start us, length us, event | category | flops | bytes accessed | tf_op | source)
XLA Modules:
  0.0 63.8 jit_solution(9967141315028611368)
XLA Ops:
  1.3 0.7 %compare_select_fusion.1 = s32[1,2]{1,0:T(1,128)S(1)} fusion(s32[1,1,2]{2,1,0:T(1,128)} %param.16, s32[]{:T(128)} %bitcast.13), kind=kLoop, calls=%fused_computation.1 | loop fusion | flops 4 | bytes 20 | tf_op jit(solution)/shard_map/jit(_where)/select_n | solution.py:332
  1.9 0.1 broadcast_bitcast_fusion
  2.0 1.1 %copy.12 = bf16[1,256,320]{2,1,0:T(8,128)(2,1)S(1)} copy(bf16[1,256,320]{1,2,0:T(8,128)(2,1)} %param.10) | data formatting | bytes 327680 | tf_op args[0]
  3.1 1.1 %copy.13 = bf16[1,256,320]{2,1,0:T(8,128)(2,1)S(1)} copy(bf16[1,256,320]{1,2,0:T(8,128)(2,1)} %param.11) | data formatting | bytes 327680 | tf_op args[1]
  4.2 0.0 copy-start
  4.2 1.3 %copy-done = bf16[1,256,2560]{2,1,0:T(8,128)(2,1)S(1)} copy-done((bf16[1,256,2560]{2,1,0:T(8,128)(2,1)S(1)}, bf16[1,256,2560]{2,1,0:T(8,128)(2,1)}, u32[]{:S(2)}) %copy-start) | copy-done | bytes 1310744
  5.5 0.0 copy-start.1
  5.5 1.1 %copy-done.1 = bf16[1,256,1280]{2,1,0:T(8,128)(2,1)S(1)} copy-done((bf16[1,256,1280]{2,1,0:T(8,128)(2,1)S(1)}, bf16[1,256,1280]{2,1,0:T(8,128)(2,1)}, u32[]{:S(2)}) %copy-start.1) | copy-done | bytes 655384
  6.6 0.0 copy-start.2
  6.6 1.1 %copy-done.2 = bf16[1,256,1280]{2,1,0:T(8,128)(2,1)S(1)} copy-done((bf16[1,256,1280]{2,1,0:T(8,128)(2,1)S(1)}, bf16[1,256,1280]{2,1,0:T(8,128)(2,1)}, u32[]{:S(2)}) %copy-start.2) | copy-done | bytes 655384
  7.7 0.0 copy-start.3
  7.7 1.1 %copy-done.3 = bf16[1,256,1280]{2,1,0:T(8,128)(2,1)S(1)} copy-done((bf16[1,256,1280]{2,1,0:T(8,128)(2,1)S(1)}, bf16[1,256,1280]{2,1,0:T(8,128)(2,1)}, u32[]{:S(2)}) %copy-start.3) | copy-done | bytes 655384
  8.8 0.0 copy-start.4
  8.8 0.9 %copy-done.4 = bf16[512,128]{1,0:T(8,128)(2,1)S(1)} copy-done((bf16[512,128]{1,0:T(8,128)(2,1)S(1)}, bf16[512,128]{1,0:T(8,128)(2,1)}, u32[]{:S(2)}) %copy-start.4) | copy-done | bytes 131096
  9.7 0.0 copy-start.5
  9.7 0.9 %copy-done.5 = bf16[320,128]{1,0:T(8,128)(2,1)S(1)} copy-done((bf16[320,128]{1,0:T(8,128)(2,1)S(1)}, bf16[320,128]{1,0:T(8,128)(2,1)}, u32[]{:S(2)}) %copy-start.5) | copy-done | bytes 81944
  10.6 51.3 %shard_map.113 = (bf16[256,2560]{1,0:T(8,128)(2,1)S(1)}, bf16[256,1280]{1,0:T(8,128)(2,1)S(1)}) custom-call(bf16[256,320]{1,0:T(8,128)(2,1)S(1)} %bitcast.17, bf16[256,320]{1,0:T(8,128)(2,1)S(1)} %bitcast.18, bf16[256,2560]{1,0:T(8,128)(2,1)S(1)} %bitcast.15, bf16[256,1280]{1,0:T(8,128)(2,1)S(1)} %bitcast.20, bf16[2,128,1280]{2,1,0:T(8,128)(2,1)S(1)} %bitcast.21, ...), custom_call_target="tpu_custom_call" | custom-call | tf_op jit(solution)/shard_map/pallas_call | solution.py:340
  61.9 1.1 %copy.17 = bf16[1,256,2560]{2,1,0:T(8,128)(2,1)} copy(bf16[1,256,2560]{2,1,0:T(8,128)(2,1)S(1)} %bitcast.16) | data formatting | bytes 2621440
  63.0 0.8 %copy.18 = bf16[1,256,1280]{2,1,0:T(8,128)(2,1)} copy(bf16[1,256,1280]{2,1,0:T(8,128)(2,1)S(1)} %bitcast.19) | data formatting | bytes 1310720
  (3 shorter events, 0.0 us)
Async XLA Ops:
  4.2 1.3 %copy-start = (bf16[1,256,2560]{2,1,0:T(8,128)(2,1)S(1)}, bf16[1,256,2560]{2,1,0:T(8,128)(2,1)}, u32[]{:S(2)}) copy-start(bf16[1,256,2560]{2,1,0:T(8,128)(2,1)} %param.12) | copy-start | bytes 3932164
  5.5 1.1 %copy-start.1 = (bf16[1,256,1280]{2,1,0:T(8,128)(2,1)S(1)}, bf16[1,256,1280]{2,1,0:T(8,128)(2,1)}, u32[]{:S(2)}) copy-start(bf16[1,256,1280]{2,1,0:T(8,128)(2,1)} %param.13) | copy-start | bytes 1966084
  6.6 1.1 %copy-start.2 = (bf16[1,256,1280]{2,1,0:T(8,128)(2,1)S(1)}, bf16[1,256,1280]{2,1,0:T(8,128)(2,1)}, u32[]{:S(2)}) copy-start(bf16[1,256,1280]{2,1,0:T(8,128)(2,1)} %param.14) | copy-start | bytes 1966084
  7.7 1.1 %copy-start.3 = (bf16[1,256,1280]{2,1,0:T(8,128)(2,1)S(1)}, bf16[1,256,1280]{2,1,0:T(8,128)(2,1)}, u32[]{:S(2)}) copy-start(bf16[1,256,1280]{2,1,0:T(8,128)(2,1)} %param.15) | copy-start | bytes 1966084
  8.8 0.9 %copy-start.4 = (bf16[512,128]{1,0:T(8,128)(2,1)S(1)}, bf16[512,128]{1,0:T(8,128)(2,1)}, u32[]{:S(2)}) copy-start(bf16[512,128]{1,0:T(8,128)(2,1)} %constant.11.clone.eq_ref) | copy-start | bytes 393220
  9.7 0.9 %copy-start.5 = (bf16[320,128]{1,0:T(8,128)(2,1)S(1)}, bf16[320,128]{1,0:T(8,128)(2,1)}, u32[]{:S(2)}) copy-start(bf16[320,128]{1,0:T(8,128)(2,1)} %constant.10.clone.ek_ref) | copy-start | bytes 245764

commit v2 on v1

--- a/solution.py
+++ b/solution.py
@@ -50,8 +50,9 @@
 
 def kernel(
     dims,
-    q_ref, k_ref, v_ref, qs_ref, ks_hbm, vs_hbm, ids_ref, bias_ref, ek_ref, eq_ref,
+    q_hbm, k_hbm, v_hbm, qs_hbm, ks_hbm, vs_hbm, sel_hbm, ids_in, count_in,
     lin_ref, soft_ref,
+    q_ref, k_ref, v_ref, qs_ref, sel_ref, ids_ref,
     kv, pieces, outgoing, imp, tbl, tbl_s, qp, kp,
     local, s_send, s_recv, n_local, n_send, n_recv, own_num, own_max, own_sum,
     load_sem, ids_send, ids_recv, p1_send, p1_recv, p2_send, p2_recv,
@@ -85,6 +86,21 @@
     load_v = pltpu.make_async_copy(vs_hbm, kv.at[:, 1], load_sem.at[1])
     load_k.start()
     load_v.start()
+    loads = [
+        pltpu.make_async_copy(a, b, load_sem.at[4 + i])
+        for i, (a, b) in enumerate((
+            (k_hbm, k_ref), (sel_hbm, sel_ref), (v_hbm, v_ref), (q_hbm, q_ref), (qs_hbm, qs_ref)))
+    ]
+    for c in loads:
+        c.start()
+    ek_ref = sel_ref.at[pl.ds(0, 2 * FPAD)]
+    eq_ref = sel_ref.at[pl.ds(2 * FPAD, 512)]
+    count = count_in[0, 0]
+    lane8 = lax.broadcasted_iota(jnp.int32, (8, 128), 1)
+    ids = jnp.zeros((8, 128), jnp.int32)
+    for i in range(maxb):
+        ids = jnp.where(lane8 == i, ids_in[0, i], ids)
+    ids_ref[...] = jnp.where(lane8 < count, ids, -1)
 
     barrier = pltpu.get_barrier_semaphore()
     for off in range(1, n):
@@ -129,8 +145,10 @@
     lanes_in = heads * FEAT
     qp[...] = jnp.zeros_like(qp)
     kp[...] = jnp.zeros_like(kp)
-    qp[:, :lanes_in] = q_ref[...]
-    kp[:, :lanes_in] = k_ref[...]
+    for c in loads:
+        c.wait()
+    qp[:, :lanes_in] = q_ref[...].T
+    kp[:, :lanes_in] = k_ref[...].T
 
     def head_tile(ref, h):
         lane = lax.broadcasted_iota(jnp.int32, (tokens, 128), 1)
@@ -238,6 +256,14 @@
 
     scale = 1.0 / math.sqrt(SM_HD)
 
+    def pairs(part, count):
+        def two(i, carry):
+            part(2 * i, 0)
+            part(2 * i + 1, 0)
+            return carry
+
+        lax.fori_loop(0, count // 2, two, 0)
+
     def own_part(h, carry):
         at = columns(h)
         for b in range(blocks):
@@ -253,7 +279,9 @@
     def imported_part(h, carry):
         at = columns(h)
         keys = imp[:, 0, :, at].reshape(maxb * BLK, SM_HD)
-        s = nt(qs_ref[:, at], keys) * scale + bias_ref[0:1, :]
+        s = nt(qs_ref[:, at], keys) * scale
+        slot = lax.broadcasted_iota(jnp.int32, (1, maxb * BLK), 1)
+        s = jnp.where(slot < count * BLK, s, -jnp.inf)
         top = jnp.maximum(own_max[h], jnp.max(s, axis=1, keepdims=True))
         p = jnp.exp(s - top)
         before = jnp.exp(own_max[h] - top)
@@ -291,12 +319,13 @@
             second.append(c)
 
     pass_on(0)
-    lax.fori_loop(0, sm_heads, own_part, 0)
+    pairs(own_part, sm_heads)
     pass_on(1)
     exchange()
-    for g in range(groups):
-        if g >= 2:
-            pass_on(g)
+    for g in range(2, groups):
+        pass_on(g)
+        lin_group(g - 2)
+    for g in range(max(groups - 2, 0), groups):
         lin_group(g)
 
     for c in second:
@@ -304,7 +333,7 @@
             c.wait()
         else:
             c.wait_recv()
-    lax.fori_loop(0, sm_heads, imported_part, 0)
+    pairs(imported_part, sm_heads)
 
     for c in id_copies + first + second[1:]:
         c.wait_send()
@@ -328,14 +357,11 @@
     kvs = 2 if sm_w % (128 * col_parts) == 0 else 1
     cols = sm_w // col_parts if kvs == 2 else sm_w * 2 // col_parts
     lanes_in = -(-heads * FEAT // 128) * 128
-    listed = jnp.arange(maxb) < import_counts[0, 0]
-    ids = jnp.pad(jnp.where(listed, import_ids[0, 0], -1)[None], ((0, 7), (0, 128 - maxb)), constant_values=-1)
-    bias = jnp.broadcast_to(
-        jnp.repeat(jnp.where(listed, 0.0, -jnp.inf).astype(F32), BLK)[None], (8, maxb * BLK))
-    for_k, for_q = selectors()
+    picks = jnp.asarray(np.concatenate(selectors()), BF16)
     dims = (n, nz, heads, sm_heads, blocks, maxb, kvs, cols)
     vmem = pl.BlockSpec(memory_space=pltpu.VMEM)
-    hbm = pl.BlockSpec(memory_space=pl.ANY)
+    hbm = pl.BlockSpec(memory_space=pltpu.HBM)
+    smem = pl.BlockSpec(memory_space=pltpu.SMEM)
     dma = pltpu.SemaphoreType.DMA
     lin, soft = pl.pallas_call(
         functools.partial(kernel, dims),
@@ -343,9 +369,15 @@
             jax.ShapeDtypeStruct((tokens, width), BF16),
             jax.ShapeDtypeStruct((tokens, sm_w), BF16),
         ),
-        in_specs=[vmem, vmem, vmem, vmem, hbm, hbm, vmem, vmem, vmem, vmem],
+        in_specs=[hbm] * 7 + [smem] * 2,
         out_specs=(vmem, vmem),
         scratch_shapes=[
+            pltpu.VMEM((heads * FEAT, tokens), BF16),
+            pltpu.VMEM((heads * FEAT, tokens), BF16),
+            pltpu.VMEM((tokens, width), BF16),
+            pltpu.VMEM((tokens, sm_w), BF16),
+            pltpu.VMEM(picks.shape, BF16),
+            pltpu.VMEM((8, 128), jnp.int32),
             pltpu.VMEM((blocks, 2, BLK, sm_w), BF16),
             pltpu.VMEM((n * blocks, kvs, ROWS, cols), BF16),
             pltpu.VMEM((n, maxb, kvs, ROWS, cols), BF16),
@@ -363,15 +395,15 @@
             pltpu.VMEM((tokens, sm_w), F32),
             pltpu.VMEM((sm_heads, tokens, 1), F32),
             pltpu.VMEM((sm_heads, tokens, 1), F32),
-            dma((4,)), dma((n,)), dma((n,)), dma((n,)), dma((n,)), dma((n,)), dma((n,)),
+            dma((9,)), dma((n,)), dma((n,)), dma((n,)), dma((n,)), dma((n,)), dma((n,)),
             dma((heads // GROUP,)), dma((heads // GROUP,)), dma, dma, dma,
         ],
         compiler_params=pltpu.CompilerParams(
-            collective_id=0, has_side_effects=True, vmem_limit_bytes=48 * 2**20),
+            collective_id=0, has_side_effects=True, vmem_limit_bytes=60 * 2**20),
     )(
-        q_lin[0], k_lin[0], v_lin[0], q_soft[0],
+        q_lin[0].T, k_lin[0].T, v_lin[0], q_soft[0],
         k_soft.reshape(blocks, BLK, sm_w), v_soft.reshape(blocks, BLK, sm_w),
-        ids, bias, jnp.asarray(for_k, BF16), jnp.asarray(for_q, BF16),
+        picks, import_ids[0], import_counts,
     )
     return lin[None], soft[None]
 

time: 64.4 us -> 57.1 us (0.89)
  local copies, waits for them, and re-layouts: 10.5 us -> 3.36 us
  Pallas kernels: 51.3 us -> 52.3 us
  other arithmetic: 0.66 us -> 0 us
    unnamed x16 -> x4, local copies, waits for them, and re-layouts: 10.4 us -> 3.36 us
    pallas_call x1, Pallas kernels: 51.3 us -> 52.3 us  [body(): pl.pallas_call(functools.partial(kernel, dims), out_shape=(jax.ShapeDtype...]
    select_n x2 -> x0, other arithmetic: 0.66 us -> none  [the longest x1 0.66 us: body(): jnp.where(listed, import_ids[0, 0], -1)[None]]
where the time goes in v2:
time: 57.1 us; the launch traced here: 57 us
  Pallas kernels  52.3 us (92%)
  local copies, waits for them, and re-layouts  3.36 us (6%)
  between operations  1.3 us (2%)
    pallas_call x1, Pallas kernels, body(): pl.pallas_call(functools.partial(kernel, dims), out_shape=(jax.ShapeDtype...  52.3 us
    unnamed x4, local copies, waits for them, and re-layouts  3.36 us

profile of v2, /device:TPU:24, one launch (start us, length us, event | category | flops | bytes accessed | tf_op | source)
XLA Modules:
  0.0 57.0 jit_solution(6735670639533029856)
XLA Ops:
  1.3 52.3 %shard_map.104 = (bf16[256,2560]{1,0:T(8,128)(2,1)}, bf16[256,1280]{1,0:T(8,128)(2,1)}) custom-call(bf16[320,256]{1,0:T(8,128)(2,1)} %bitcast.19, bf16[320,256]{1,0:T(8,128)(2,1)} %bitcast.20, bf16[256,2560]{1,0:T(8,128)(2,1)} %bitcast.13, bf16[256,1280]{1,0:T(8,128)(2,1)} %bitcast.16, bf16[2,128,1280]{2,1,0:T(8,128)(2,1)} %bitcast.17, ...), custom_call_target="tpu_custom_call" | custom-call | tf_op jit(solution)/shard_map/pallas_call | solution.py:366
  53.6 0.0 copy-start
  53.6 2.5 %copy.14 = bf16[1,256,2560]{2,1,0:T(8,128)(2,1)} copy(bf16[1,256,2560]{2,1,0:T(8,128)(2,1)} %bitcast.14) | data formatting | bytes 2621440
  56.1 0.0 copy-done
  56.1 0.8 %copy.15 = bf16[1,256,1280]{2,1,0:T(8,128)(2,1)} copy(bf16[1,256,1280]{2,1,0:T(8,128)(2,1)S(1)} %bitcast.15) | data formatting | bytes 1310720
Async XLA Ops:
  53.6 2.5 %copy-start = (bf16[256,1280]{1,0:T(8,128)(2,1)S(1)}, bf16[256,1280]{1,0:T(8,128)(2,1)}, u32[]{:S(2)}) copy-start(bf16[256,1280]{1,0:T(8,128)(2,1)} %get-tuple-element.5) | copy-start | bytes 1966084

commit v3 on v2

--- a/solution.py
+++ b/solution.py
@@ -16,7 +16,7 @@
 SM_HD = 128
 BLK = 128
 ROWS = 16
-GROUP = 4
+GROUP = 2
 MESH = pl.DeviceIdType.MESH
 F32 = jnp.float32
 BF16 = jnp.bfloat16
@@ -53,10 +53,10 @@
     q_hbm, k_hbm, v_hbm, qs_hbm, ks_hbm, vs_hbm, sel_hbm, ids_in, count_in,
     lin_ref, soft_ref,
     q_ref, k_ref, v_ref, qs_ref, sel_ref, ids_ref,
-    kv, pieces, outgoing, imp, tbl, tbl_s, qp, kp,
+    kv, pieces_a, pieces_b, outgoing, imp, tbl, tbl_s, qp, kp,
     local, s_send, s_recv, n_local, n_send, n_recv, own_num, own_max, own_sum,
     load_sem, ids_send, ids_recv, p1_send, p1_recv, p2_send, p2_recv,
-    st_send, st_recv, nm_send, nm_recv, tbl_sem,
+    st_send, st_recv, nm_send, nm_recv, tbl_sem, own_sem,
 ):
     n, nz, heads, sm_heads, blocks, maxb, kvs, cols = dims
     tokens = blocks * BLK
@@ -127,20 +127,33 @@
     tbl[me] = ids_ref[...]
     load_k.wait()
     load_v.wait()
+    parts = 2 if cols % 256 == 0 else 1
+    pieces = (pieces_a, pieces_b)
+    width = cols // parts
+
+    def cut(p, c):
+        at_kv, at_row, at_col = piece(p)
+        at_col = pl.ds(pl.multiple_of(at_col.start + c * width, 128), width)
+        return at_kv, at_row, at_col
+
     first = []
-    for off in range(1, n):
-        to = peer(off)
-        at_kv, at_row, at_col = piece(to)
-        c = pltpu.make_async_remote_copy(
-            src_ref=kv.at[:, at_kv, at_row, at_col], dst_ref=pieces.at[pl.ds(me * blocks, blocks)],
-            send_sem=p1_send.at[off], recv_sem=p1_recv.at[off],
-            device_id={"files": to}, device_id_type=MESH)
-        c.start()
-        first.append(c)
-    at_kv, at_row, at_col = piece(me)
-    mine = pltpu.make_async_copy(
-        kv.at[:, at_kv, at_row, at_col], pieces.at[pl.ds(me * blocks, blocks)], load_sem.at[2])
-    mine.start()
+    for c in range(parts):
+        for off in range(1, n):
+            to = peer(off)
+            at_kv, at_row, at_col = cut(to, c)
+            copy = pltpu.make_async_remote_copy(
+                src_ref=kv.at[:, at_kv, at_row, at_col], dst_ref=pieces[c].at[pl.ds(me * blocks, blocks)],
+                send_sem=p1_send.at[c, off], recv_sem=p1_recv.at[c, off],
+                device_id={"files": to}, device_id_type=MESH)
+            copy.start()
+            first.append(copy)
+    mine = []
+    for c in range(parts):
+        at_kv, at_row, at_col = cut(me, c)
+        copy = pltpu.make_async_copy(
+            kv.at[:, at_kv, at_row, at_col], pieces[c].at[pl.ds(me * blocks, blocks)], own_sem.at[0, c])
+        copy.start()
+        mine.append(copy)
 
     lanes_in = heads * FEAT
     qp[...] = jnp.zeros_like(qp)
@@ -177,12 +190,6 @@
         local[h] = made[:, :HD]
         return made[:, HD:]
 
-    def states(i, carry):
-        n_local[...] += state_of(2 * i) + state_of(2 * i + 1)
-        return carry
-
-    lax.fori_loop(0, heads // 2, states, 0)
-
     groups = heads // GROUP
 
     def norm_copy():
@@ -196,29 +203,42 @@
             src_ref=s_send.at[at], dst_ref=s_recv.at[at], send_sem=st_send.at[g], recv_sem=st_recv.at[g],
             device_id={"seq": lax.rem(z + 1, nz)}, device_id_type=MESH)
 
+    def states(i, carry):
+        n_local[...] += state_of(2 * i) + state_of(2 * i + 1)
+
+        @pl.when(z == 0)
+        def _():
+            at = pl.ds(2 * i, GROUP)
+            s_send[at] = local[at].astype(BF16)
+            state_copy(i).start()
+
+        return carry
+
+    lax.fori_loop(0, groups, states, 0)
+
     @pl.when(z == 0)
     def _():
         n_recv[...] = jnp.zeros_like(n_recv)
         s_recv[...] = jnp.zeros_like(s_recv)
-
-    @pl.when(has_prev)
-    def _():
-        norm_copy().wait_recv()
-
-    @pl.when(has_next)
-    def _():
-        n_send[...] = n_recv[...] + n_local[...]
+        n_send[...] = n_local[...]
         norm_copy().start()
 
-    def pass_on(g):
-        at = pl.ds(g * GROUP, GROUP)
-
+    def forward_norm():
         @pl.when(has_prev)
         def _():
+            norm_copy().wait_recv()
+
+        @pl.when(has_prev & has_next)
+        def _():
+            n_send[...] = n_recv[...] + n_local[...]
+            norm_copy().start()
+
+    def forward(g, here):
+        at = pl.ds(g * GROUP, GROUP)
+
+        @pl.when(has_prev & has_next & here)
+        def _():
             state_copy(g).wait_recv()
-
-        @pl.when(has_next)
-        def _():
             s_send[at] = (s_recv[at].astype(F32) + local[at]).astype(BF16)
             state_copy(g).start()
 
@@ -240,6 +260,10 @@
         lin_ref[:, columns(h)] = ((num + far[:, :HD]) / den).astype(BF16)
 
     def lin_group(g):
+        @pl.when(z == nz - 1)
+        def _():
+            state_copy(g).wait_recv()
+
         total = n_recv[...]
         high = total.astype(BF16)
         low = (total - high.astype(F32)).astype(BF16)
@@ -256,13 +280,15 @@
 
     scale = 1.0 / math.sqrt(SM_HD)
 
-    def pairs(part, count):
+    def pairs(part, low, high):
         def two(i, carry):
-            part(2 * i, 0)
-            part(2 * i + 1, 0)
+            part(low + 2 * i, 0)
+            part(low + 2 * i + 1, 0)
             return carry
 
-        lax.fori_loop(0, count // 2, two, 0)
+        lax.fori_loop(0, (high - low) // 2, two, 0)
+        if (high - low) % 2:
+            part(high - 1, 0)
 
     def own_part(h, carry):
         at = columns(h)
@@ -291,52 +317,65 @@
         soft_ref[:, at] = (num / total).astype(BF16)
         return carry
 
-    second = []
-
-    def exchange():
-        for c in id_copies:
-            c.wait_recv()
-        to_smem = pltpu.make_async_copy(tbl, tbl_s, tbl_sem)
-        to_smem.start()
-        to_smem.wait()
-        for c in first:
-            c.wait_recv()
-        mine.wait()
-        at_kv, at_row, at_col = piece(me)
-        for off in range(n):
+    second = [[] for _ in range(parts)]
+
+    def exchange(c):
+        if c == 0:
+            for copy in id_copies:
+                copy.wait_recv()
+            to_smem = pltpu.make_async_copy(tbl, tbl_s, tbl_sem)
+            to_smem.start()
+            to_smem.wait()
+        for copy in first[c * (n - 1):(c + 1) * (n - 1)]:
+            copy.wait_recv()
+        mine[c].wait()
+        at_kv, at_row, at_col = cut(me, c)
+        there = imp.at[:, at_kv, at_row, at_col]
+        for off in list(range(1, n)) + [0]:
             to = peer(off)
             for i in range(maxb):
-                outgoing[off, i] = pieces[jnp.maximum(tbl_s[to, 0, i], 0)]
-            there = imp.at[:, at_kv, at_row, at_col]
+                outgoing[c, off, i] = pieces[c][jnp.maximum(tbl_s[to, 0, i], 0)]
             if off == 0:
-                c = pltpu.make_async_copy(outgoing.at[0], there, load_sem.at[3])
+                copy = pltpu.make_async_copy(outgoing.at[c, 0], there, own_sem.at[1, c])
             else:
-                c = pltpu.make_async_remote_copy(
-                    src_ref=outgoing.at[off], dst_ref=there,
-                    send_sem=p2_send.at[off], recv_sem=p2_recv.at[off],
+                copy = pltpu.make_async_remote_copy(
+                    src_ref=outgoing.at[c, off], dst_ref=there,
+                    send_sem=p2_send.at[c, off], recv_sem=p2_recv.at[c, off],
                     device_id={"files": to}, device_id_type=MESH)
-            c.start()
-            second.append(c)
-
-    pass_on(0)
-    pairs(own_part, sm_heads)
-    pass_on(1)
-    exchange()
+            copy.start()
+            second[c].append(copy)
+
+    always = z >= 0
+    pairs(own_part, 0, sm_heads)
+    exchange(0)
+    forward_norm()
+    forward(0, z < 3)
+    forward(1, z < 2)
+    for c in range(1, parts):
+        exchange(c)
+    forward(0, z >= 3)
+    forward(1, z >= 2)
     for g in range(2, groups):
-        pass_on(g)
-        lin_group(g - 2)
-    for g in range(max(groups - 2, 0), groups):
+        forward(g, always)
+        if g >= 4:
+            lin_group(g - 4)
+    for g in range(groups - 4, groups):
         lin_group(g)
 
-    for c in second:
-        if c is second[0]:
-            c.wait()
-        else:
-            c.wait_recv()
-    pairs(imported_part, sm_heads)
-
-    for c in id_copies + first + second[1:]:
-        c.wait_send()
+    for c in range(parts):
+        for copy in second[c][:-1]:
+            copy.wait_recv()
+        second[c][-1].wait()
+        if parts == 2:
+            pairs(imported_part, c * sm_heads // 2, (c + 1) * sm_heads // 2)
+    if parts == 1:
+        pairs(imported_part, 0, sm_heads)
+
+    for copy in id_copies + first:
+        copy.wait_send()
+    for c in range(parts):
+        for copy in second[c][:-1]:
+            copy.wait_send()
 
     @pl.when(has_next)
     def _():
@@ -356,6 +395,7 @@
     col_parts = n * ROWS // BLK
     kvs = 2 if sm_w % (128 * col_parts) == 0 else 1
     cols = sm_w // col_parts if kvs == 2 else sm_w * 2 // col_parts
+    parts = 2 if cols % 256 == 0 else 1
     lanes_in = -(-heads * FEAT // 128) * 128
     picks = jnp.asarray(np.concatenate(selectors()), BF16)
     dims = (n, nz, heads, sm_heads, blocks, maxb, kvs, cols)
@@ -379,8 +419,9 @@
             pltpu.VMEM(picks.shape, BF16),
             pltpu.VMEM((8, 128), jnp.int32),
             pltpu.VMEM((blocks, 2, BLK, sm_w), BF16),
-            pltpu.VMEM((n * blocks, kvs, ROWS, cols), BF16),
-            pltpu.VMEM((n, maxb, kvs, ROWS, cols), BF16),
+            pltpu.VMEM((n * blocks, kvs, ROWS, cols // parts), BF16),
+            pltpu.VMEM((n * blocks if parts == 2 else 1, kvs, ROWS, cols // parts), BF16),
+            pltpu.VMEM((parts, n, maxb, kvs, ROWS, cols // parts), BF16),
             pltpu.VMEM((maxb, 2, BLK, sm_w), BF16),
             pltpu.VMEM((n, 8, 128), jnp.int32),
             pltpu.SMEM((n, 8, 128), jnp.int32),
@@ -395,8 +436,8 @@
             pltpu.VMEM((tokens, sm_w), F32),
             pltpu.VMEM((sm_heads, tokens, 1), F32),
             pltpu.VMEM((sm_heads, tokens, 1), F32),
-            dma((9,)), dma((n,)), dma((n,)), dma((n,)), dma((n,)), dma((n,)), dma((n,)),
-            dma((heads // GROUP,)), dma((heads // GROUP,)), dma, dma, dma,
+            dma((9,)), dma((n,)), dma((n,)), dma((parts, n)), dma((parts, n)), dma((parts, n)), dma((parts, n)),
+            dma((heads // GROUP,)), dma((heads // GROUP,)), dma, dma, dma, dma((2, parts)),
         ],
         compiler_params=pltpu.CompilerParams(
             collective_id=0, has_side_effects=True, vmem_limit_bytes=60 * 2**20),

time: 57.1 us -> 60.6 us (1.061)
  Pallas kernels: 52.3 us -> 55.8 us
    pallas_call x1, Pallas kernels: 52.3 us -> 55.8 us  [body(): pl.pallas_call(functools.partial(kernel, dims), out_shape=(jax.ShapeDtype...]
where the time goes in v3:
time: 60.6 us; the launch traced here: 60.4 us
  Pallas kernels  55.8 us (92%)
  local copies, waits for them, and re-layouts  3.36 us (6%)
  between operations  1.3 us (2%)
    pallas_call x1, Pallas kernels, body(): pl.pallas_call(functools.partial(kernel, dims), out_shape=(jax.ShapeDtype...  55.8 us
    unnamed x4, local copies, waits for them, and re-layouts  3.36 us

profile of v3, /device:TPU:24, one launch (start us, length us, event | category | flops | bytes accessed | tf_op | source)
XLA Modules:
  0.0 60.4 jit_solution(4796766197870106406)
XLA Ops:
  1.3 55.8 %shard_map.104 = (bf16[256,2560]{1,0:T(8,128)(2,1)}, bf16[256,1280]{1,0:T(8,128)(2,1)}) custom-call(bf16[320,256]{1,0:T(8,128)(2,1)} %bitcast.19, bf16[320,256]{1,0:T(8,128)(2,1)} %bitcast.20, bf16[256,2560]{1,0:T(8,128)(2,1)} %bitcast.13, bf16[256,1280]{1,0:T(8,128)(2,1)} %bitcast.16, bf16[2,128,1280]{2,1,0:T(8,128)(2,1)} %bitcast.17, ...), custom_call_target="tpu_custom_call" | custom-call | tf_op jit(solution)/shard_map/pallas_call | solution.py:406
  57.1 0.0 copy-start
  57.1 2.5 %copy.14 = bf16[1,256,2560]{2,1,0:T(8,128)(2,1)} copy(bf16[1,256,2560]{2,1,0:T(8,128)(2,1)} %bitcast.14) | data formatting | bytes 2621440
  59.6 0.0 copy-done
  59.6 0.8 %copy.15 = bf16[1,256,1280]{2,1,0:T(8,128)(2,1)} copy(bf16[1,256,1280]{2,1,0:T(8,128)(2,1)S(1)} %bitcast.15) | data formatting | bytes 1310720
Async XLA Ops:
  57.1 2.5 %copy-start = (bf16[256,1280]{1,0:T(8,128)(2,1)S(1)}, bf16[256,1280]{1,0:T(8,128)(2,1)}, u32[]{:S(2)}) copy-start(bf16[256,1280]{1,0:T(8,128)(2,1)} %get-tuple-element.5) | copy-start | bytes 1966084
